TPU v7x, 256 devices: a whole 4x4x8 slice. The times are simulated.
256 devices in a mesh: row: 32 (over z, x_lo, core), col: 8 (over x_hi, y).
Axes of the slice: x: 4 (x_hi: 2, x_lo: 2; x = x_hi * 2 + x_lo), y: 4, z: 8, core: 2. Of those that a mesh axis runs over, the one named last changes fastest.
Arguments:
- images: bfloat16 [16384, 1152], P(('row', 'col')), may hold values from -8 to 8
- texts: bfloat16 [16384, 1152], P(('row', 'col')), may hold values from -8 to 8
- log_scale: float32 [1], replicated, may hold values from 1.8 to 3
- bias: float32 [1], replicated, may hold values from -12 to -6
Outputs:
- image_grad: float32 [16384, 1152], P(('row', 'col'))
- text_grad: float32 [16384, 1152], P(('row', 'col'))
- loss: float32 [1], replicated
- log_scale_grad: float32 [1], replicated
- bias_grad: float32 [1], replicated
All inputs are finite; a program needn't handle non-finite values.
Results may differ from a plain program's by a relative error of at most 0.002.
The roundings to bfloat16 on the way count: a program that leaves them out, or rounds other values in their place, can miss the bound.
Values may be sent and summed in bfloat16 or wider, within the bound.
A program may use at most 64 MiB of HBM per device.

v0:
```python
import jax
import jax.numpy as jnp
from jax import lax
from jax.experimental import pallas as pl
from jax.experimental.pallas import tpu as pltpu
from jax.sharding import PartitionSpec as P

MESH = pl.DeviceIdType.MESH
F32 = jnp.float32
BF16 = jnp.bfloat16
ROWS = 64
QUARTER = 16
HALF = 32
WIDTH = 1152
PAIRS = 16384
LOG2E = 1.4426950408889634
TILE = 1024

GATHER_PARTS = (
    ((0, 1),),
    ((0, 1), (1, 2)),
    ((0, 1), (1, 2), (2, 4)),
    ((0, 1), (1, 2), (2, 4), (4, 8)),
)
REDUCE_PARTS = (
    ((1, 2),),
    ((3, 4), (2, 3)),
    ((6, 8), (5, 6), (4, 5)),
    ((12, 16), (10, 12), (9, 10), (8, 9)),
)
FIRST_PART = (0, 1, 3, 6)
UP = {0: 0, 1: 2, 2: 4, 3: 6, 4: 7}
DOWN = {0: 0, 1: 1, 2: 3, 3: 5, 4: 7}


def unit_rows(raw):
    values = raw[...].astype(F32)
    inverse = lax.rsqrt(jnp.sum(values * values, axis=1, keepdims=True) + 1e-06)
    return values * inverse, inverse


def encode(v):
    squared = v * v
    return (v * jnp.abs(v) * squared).astype(BF16)


def decode(y):
    y = y.astype(F32)
    root = lax.rsqrt(lax.rsqrt(jnp.maximum(jnp.abs(y), 1e-37)))
    return jnp.where(y > 0.0, root, jnp.where(y < 0.0, -root, 0.0))


def kernel(
    images_in, texts_in, log_scale, bias,
    image_sum, text_sum, stat_sum,
    img, txt, w, iacc, tacc, isend, irecv, csend, crecv, tsend, trecv, stat, acc,
    gi_s, gi_r, gt_s, gt_r, gc_s, gc_r, ri_s, ri_r, rc_s, rc_r, rt_s, rt_r, st_s, st_r, images, texts, in_s,
):
    row = lax.axis_index("row")
    col = lax.axis_index("col")
    x = 2 * (col // 4) + (row // 2) % 2
    y = col % 4
    z = row // 4
    core = row % 2

    def device(x, y, z, core):
        return (z * 4 + (x % 2) * 2 + core, (x // 2) * 4 + y)

    x_flip = x + 1 - 2 * (x % 2)
    y_flip = y + 1 - 2 * (y % 2)
    plane = (
        device(x_flip, y, z, core),
        device(x, y_flip, z, core),
        device(3 - x, y, z, core),
        device(x, 3 - y, z, core),
    )
    above = device(x, y, (z + 1) % 8, core)
    below = device(x, y, (z + 7) % 8, core)
    sibling = device(x, y, z, 1 - core)

    barrier = pltpu.get_barrier_semaphore()
    for other in (*plane, above, below, sibling):
        pl.semaphore_signal(barrier, inc=1, device_id=other, device_id_type=MESH)

    inputs = [
        pltpu.make_async_copy(src, dst, in_s.at[i])
        for i, (src, dst) in enumerate(((images_in, images), (texts_in, texts)))
    ]
    for c in inputs:
        c.start()
    sent = []

    def copy(src, dst, send, recv, to):
        return pltpu.make_async_remote_copy(
            src_ref=src, dst_ref=dst, send_sem=send, recv_sem=recv, device_id=to, device_id_type=MESH
        )

    def start(c):
        c.start()
        sent.append(c)

    def gather_image(q, s, part):
        a, b = GATHER_PARTS[s][part]
        n = FIRST_PART[s] + part
        return copy(
            img.at[a:b, q], img.at[2**s + a : 2**s + b, q], gi_s.at[q, n], gi_r.at[q, n], plane[(q + s) % 4]
        )

    def gather_text(way, step, half):
        slots = (UP, DOWN)[way]
        src, dst = slots[step], slots[step + 1]
        rows = slice(half * HALF, (half + 1) * HALF)
        return copy(
            txt.at[src, 0, rows], txt.at[dst, 0, rows],
            gt_s.at[way, step, half], gt_r.at[way, step, half], (above, below)[way],
        )

    def share_text(slot, half):
        rows = slice(half * HALF, (half + 1) * HALF)
        return copy(txt.at[slot, 0, rows], txt.at[slot, 1, rows], gc_s.at[slot, half], gc_r.at[slot, half], sibling)

    def reduce_image(q, s, part):
        a, b = REDUCE_PARTS[s][part]
        n = FIRST_PART[s] + part
        return copy(isend.at[a:b, q], irecv.at[a:b, q], ri_s.at[q, n], ri_r.at[q, n], plane[(q + s) % 4])

    def share_sum(slot):
        return copy(csend.at[slot], crecv.at[slot], rc_s.at[slot], rc_r.at[slot], sibling)

    def reduce_text(way, m, half):
        rows = slice(half * HALF, (half + 1) * HALF)
        return copy(
            tsend.at[way, m, rows], trecv.at[way, m, rows],
            rt_s.at[way, m, half], rt_r.at[way, m, half], (above, below)[way],
        )

    def send_stat(n, src, to):
        return copy(stat.at[src], stat.at[n], st_s.at[n], st_r.at[n], to)

    inputs[0].wait()
    img[0] = unit_rows(images)[0].astype(BF16).reshape(4, QUARTER, WIDTH)
    inputs[1].wait()
    txt[0, 0] = unit_rows(texts)[0].astype(BF16)
    scale = jnp.exp(log_scale[...])
    shift = bias[...]
    scale_two = scale * LOG2E
    shift_two = shift * LOG2E
    acc[...] = jnp.zeros_like(acc)
    pl.semaphore_wait(barrier, 7)

    def block(first_row, rows, first_col, columns):
        c = lax.dot_general(
            img[pl.ds(first_row // 64, rows // 64)].reshape(rows, WIDTH),
            txt[first_col // 128 : (first_col + columns) // 128].reshape(columns, WIDTH),
            (((1,), (1,)), ((), ())),
            preferred_element_type=F32,
        )
        e = jnp.exp2(c * scale_two + shift_two)
        gate = e / (1.0 + e)
        w[pl.ds(first_row, rows), first_col : first_col + columns] = (scale * gate).astype(BF16)

        def fold(v):
            v = jnp.sum(v.reshape(-1, 16, columns), axis=0)
            return sum(v[:, k : k + 128] for k in range(0, columns, 128))

        fourth = rows // 4
        a, b = e[: 2 * fourth], e[2 * fourth :]
        a = a + b + a * b
        a, b = a[:fourth], a[fourth:]
        acc[0] = acc[0] + fold(jnp.log1p(a + b + a * b))
        acc[1] = acc[1] + fold(gate * c)
        acc[2] = acc[2] + fold(gate)

    def blocks(first_slot, end_slot, first_text, end_text):
        def one(i, _):
            block(pl.multiple_of(first_slot * 64 + i * 256, 256), 256, first_text * 128, (end_text - first_text) * 128)
            return 0

        lax.fori_loop(0, (end_slot - first_slot) // 4, one, 0)

    def own_pairs():
        c = lax.dot_general(
            img[0].reshape(ROWS, WIDTH),
            txt[0].reshape(2 * ROWS, WIDTH),
            (((1,), (1,)), ((), ())),
            preferred_element_type=F32,
        )
        logit = scale * c + shift
        same = lax.broadcasted_iota(jnp.int32, (ROWS, 128), 0) == lax.broadcasted_iota(jnp.int32, (ROWS, 128), 1)
        match = -scale / (1.0 + jnp.exp(logit))
        w[:ROWS, :128] = jnp.where(same, match, w[:ROWS, :128].astype(F32)).astype(BF16)
        for k, v in enumerate((logit, c, jnp.ones_like(c))):
            acc[k] = acc[k] - jnp.where(same, v, 0.0).reshape(4, 16, 128).sum(axis=0)

    for s in range(4):
        for q in range(4):
            start(gather_image(q, s, 0))
        if s < 2:
            for way in range(2):
                start(gather_text(way, 0, s if way == 0 else 1 - s))
    for half in range(2):
        start(share_text(0, half))

    def pass_text(way, step, half):
        gather_text(way, step, half).wait_recv()
        slot = (UP, DOWN)[way][step + 1]
        if step < 2 or (step == 2 and half == way):
            start(gather_text(way, step + 1, half))
        start(share_text(slot, half))

    def got_image(s, part):
        for q in range(4):
            gather_image(q, s, part).wait_recv()

    def pass_image(stages, part):
        for s in stages:
            for q in range(4):
                start(gather_image(q, s, part))

    def got_shared(slots):
        for slot in slots:
            for half in range(2):
                share_text(slot, half).wait_recv()

    got_image(0, 0)
    pass_image((1, 2, 3), 1)
    for way in range(2):
        pass_text(way, 0, way)
    got_image(1, 0)
    got_image(1, 1)
    pass_image((2, 3), 2)
    for way in range(2):
        pass_text(way, 0, 1 - way)
    got_shared((0, 1, 2))
    blocks(0, 4, 0, 3)
    own_pairs()
    for way in range(2):
        pass_text(way, 1, way)
    for way in range(2):
        pass_text(way, 1, 1 - way)
    for part in range(3):
        got_image(2, part)
    pass_image((3,), 3)
    blocks(4, 8, 0, 3)
    got_shared((3, 4))
    for way in range(2):
        pass_text(way, 2, way)
    blocks(0, 8, 3, 5)
    for way in range(2):
        pass_text(way, 2, 1 - way)
    for part in range(3):
        got_image(3, part)
    blocks(8, 12, 0, 5)
    got_shared((5, 6))
    blocks(0, 4, 5, 7)
    for way in range(2):
        pass_text(way, 3, way)
    blocks(4, 12, 5, 7)
    got_shared((7,))
    got_image(3, 3)
    blocks(12, 16, 0, 8)

    def stat_plane(n):
        return send_stat(n, 0, device((x + n // 4) % 4, (y + n % 4) % 4, z, core))

    def stat_column(n):
        return send_stat(16 + n, 16, device(x, y, (z + n // 2) % 8, (core + n) % 2))

    def stat_own():
        stat[0] = jnp.zeros((8, 128), F32)
        for k in range(3):
            stat[0, k : k + 1] = jnp.sum(acc[k], axis=0, keepdims=True)
        for n in range(1, 16):
            start(stat_plane(n))

    def stat_turn():
        total = stat[0]
        for n in range(1, 16):
            stat_plane(n).wait_recv()
            total = total + stat[n]
        stat[16] = total
        for n in range(1, 16):
            start(stat_column(n))

    def stat_last():
        total = stat[16]
        for n in range(1, 16):
            stat_column(n).wait_recv()
            total = total + stat[16 + n]
        stat_sum[...] = total

    def image_part(slot):
        return jnp.dot(
            w[slot * 64 : (slot + 4) * 64, :], txt[...].reshape(TILE, WIDTH), preferred_element_type=F32
        ).reshape(4, 4, QUARTER, WIDTH)

    def text_part(slot, count):
        part = lax.dot_general(
            w[:, slot * 128 : (slot + count) * 128],
            img[...].reshape(TILE, WIDTH),
            (((0,), (0,)), ((), ())),
            preferred_element_type=F32,
        ).reshape(count, 2, ROWS, WIDTH)
        csend[slot : slot + count] = encode(part[:, 1])
        tacc[slot : slot + count] = part[:, 0]
        for k in range(slot, slot + count):
            start(share_sum(k))

    def send_images(s, parts):
        for part in parts:
            for q in range(4):
                start(reduce_image(q, s, part))

    def wait_images(s, part):
        for q in range(4):
            reduce_image(q, s, part).wait_recv()

    def add_images(first, count, stage, forward):
        def one(i, _):
            slot, q = first + i // 4, i % 4
            total = iacc[slot, q] + decode(irecv[2**stage + slot, q])
            if forward:
                isend[slot, q] = encode(total)
            else:
                iacc[slot, q] = total
            return 0

        lax.fori_loop(0, 4 * count, one, 0)

    def join_texts(slot):
        share_sum(slot).wait_recv()

        def one(i, _):
            rows = pl.ds(pl.multiple_of(i * 16, 16), 16)
            tacc[slot, rows] = tacc[slot, rows] + decode(crecv[slot, rows])
            return 0

        lax.fori_loop(0, 4, one, 0)

    def pass_sum(way, m, half):
        slot = (DOWN, UP)[way][m]
        arrives = m == 3 and half == way or m < 3
        if arrives:
            reduce_text(way, m + 1, half).wait_recv()
        for i in range(2):
            rows = slice(half * HALF + i * 16, half * HALF + (i + 1) * 16)
            total = tacc[slot, rows]
            if arrives:
                total = total + decode(trecv[way, m + 1, rows])
            tsend[way, m, rows] = encode(total)
        start(reduce_text(way, m, half))

    def pass_sums(m, own):
        for way in range(2):
            pass_sum(way, m, way if own else 1 - way)

    isend[12:16] = encode(image_part(12))
    send_images(3, (0,))
    block(0, 768, 896, 128)
    text_part(7, 1)
    stat_own()
    text_part(5, 2)
    join_texts(7)
    pass_sums(4, True)
    isend[8:12] = encode(image_part(8))
    send_images(3, (1, 2, 3))
    join_texts(5)
    join_texts(6)
    pass_sums(3, False)
    text_part(3, 2)
    iacc[4:8] = image_part(4)
    pass_sums(3, True)
    join_texts(3)
    join_texts(4)
    pass_sums(2, False)
    wait_images(3, 0)
    add_images(4, 4, 3, True)
    send_images(2, (0, 1, 2))
    stat_turn()
    iacc[0:4] = image_part(0)
    text_part(0, 3)
    pass_sums(2, True)
    for part in (1, 2, 3):
        wait_images(3, part)
    add_images(0, 4, 3, False)
    for slot in (1, 2, 0):
        join_texts(slot)
    wait_images(2, 0)
    add_images(2, 2, 2, True)
    send_images(1, (0, 1))
    pass_sums(1, False)
    wait_images(2, 1)
    wait_images(2, 2)
    add_images(0, 2, 2, False)
    pass_sums(1, True)
    wait_images(1, 0)
    add_images(1, 1, 1, True)
    send_images(0, (0,))
    wait_images(1, 1)
    add_images(0, 1, 1, False)
    stat_last()

    for way in range(2):
        for half in range(2):
            reduce_text(way, 1, half).wait_recv()
    text_sum[...] = tacc[0] + decode(trecv[0, 1]) + decode(trecv[1, 1])
    wait_images(0, 0)
    image_sum[...] = (iacc[0] + decode(irecv[1])).reshape(ROWS, WIDTH)
    for c in sent:
        c.wait_send()


def finish(images, texts, image_sum, text_sum, stat_sum, log_scale, image_grad, text_grad, loss, scale_grad, bias_grad):
    for raw, total, out in ((images, image_sum, image_grad), (texts, text_sum, text_grad)):
        unit, inverse = unit_rows(raw)
        grad = total[...] * (1.0 / PAIRS)
        out[...] = inverse * (grad - unit * jnp.sum(unit * grad, axis=1, keepdims=True))
    scale = jnp.exp(jnp.broadcast_to(log_scale[...], (1, 128)))
    loss[0] = jnp.sum(stat_sum[0:1]) * (1.0 / PAIRS)
    scale_grad[0] = jnp.sum(stat_sum[1:2] * scale) * (1.0 / PAIRS)
    bias_grad[0] = jnp.sum(stat_sum[2:3]) * (1.0 / PAIRS)


def body(images, texts, log_scale, bias):
    vmem = pl.BlockSpec(memory_space=pltpu.VMEM)
    smem = pl.BlockSpec(memory_space=pltpu.SMEM)
    dma = pltpu.SemaphoreType.DMA
    grad = jax.ShapeDtypeStruct((ROWS, WIDTH), F32)
    scalar = jax.ShapeDtypeStruct((1,), F32)
    log_scale = log_scale.reshape(1, 1)
    image_sum, text_sum, stat_sum = pl.pallas_call(
        kernel,
        out_shape=(grad, grad, jax.ShapeDtypeStruct((8, 128), F32)),
        in_specs=[pl.BlockSpec(memory_space=pl.ANY)] * 2 + [vmem] * 2,
        out_specs=(vmem,) * 3,
        scratch_shapes=[
            pltpu.VMEM((16, 4, QUARTER, WIDTH), BF16),
            pltpu.VMEM((8, 2, ROWS, WIDTH), BF16),
            pltpu.VMEM((TILE, TILE), BF16),
            pltpu.VMEM((8, 4, QUARTER, WIDTH), F32),
            pltpu.VMEM((8, ROWS, WIDTH), F32),
            pltpu.VMEM((16, 4, QUARTER, WIDTH), BF16),
            pltpu.VMEM((16, 4, QUARTER, WIDTH), BF16),
            pltpu.VMEM((8, ROWS, WIDTH), BF16),
            pltpu.VMEM((8, ROWS, WIDTH), BF16),
            pltpu.VMEM((2, 5, ROWS, WIDTH), BF16),
            pltpu.VMEM((2, 5, ROWS, WIDTH), BF16),
            pltpu.VMEM((33, 8, 128), F32),
            pltpu.VMEM((3, 16, 128), F32),
            dma((4, 10)), dma((4, 10)),
            dma((2, 4, 2)), dma((2, 4, 2)),
            dma((8, 2)), dma((8, 2)),
            dma((4, 10)), dma((4, 10)),
            dma((8,)), dma((8,)),
            dma((2, 5, 2)), dma((2, 5, 2)),
            dma((32,)), dma((32,)),
            pltpu.VMEM((ROWS, WIDTH), BF16), pltpu.VMEM((ROWS, WIDTH), BF16), dma((2,)),
        ],
        compiler_params=pltpu.CompilerParams(
            collective_id=0, has_side_effects=True, vmem_limit_bytes=56 * 2**20
        ),
        cost_estimate=pl.CostEstimate(flops=6 * TILE * TILE * WIDTH, bytes_accessed=2**20, transcendentals=2 * TILE * TILE),
        name="pairs",
    )(images, texts, log_scale, bias.reshape(1, 1))
    return pl.pallas_call(
        finish,
        out_shape=(grad, grad, scalar, scalar, scalar),
        in_specs=[vmem] * 6,
        out_specs=(vmem, vmem, smem, smem, smem),
        name="finish",
    )(images, texts, image_sum, text_sum, stat_sum, log_scale)


def solution(mesh):
    rows = P(("row", "col"), None)
    return jax.shard_map(
        body,
        mesh=mesh,
        in_specs=(rows, rows, P(), P()),
        out_specs=(rows, rows, P(), P(), P()),
        check_vma=False,
    )
```

profile of v0, /device:TPU:1, one launch (start us, length us, event | category | flops | bytes accessed | tf_op | source)
XLA Modules:
  0.0 58.8 jit_solution(3673798763712980813)
XLA Ops:
  1.9 54.6 %pairs.1 = (f32[64,1152]{1,0:T(8,128)}, f32[64,1152]{1,0:T(8,128)}, f32[8,128]{1,0:T(8,128)}) custom-call(bf16[64,1152]{1,0:T(8,128)(2,1)} %images.1, bf16[64,1152]{1,0:T(8,128)(2,1)} %texts.1, f32[1,1]{1,0:T(1,128)} %bitcast.2.log_scale, f32[1,1]{1,0:T(1,128)} %bitcast.4.bias), custom_call_target="tpu_custom_call" | custom-call | flops 7247757312 | bytes 1048576 | tf_op jit(solution)/shard_map/pairs/pallas_call | solution.py:431
  56.5 2.3 %finish.1 = (f32[64,1152]{1,0:T(8,128)}, f32[64,1152]{1,0:T(8,128)}, f32[1]{0:T(128)}, f32[1]{0:T(128)}, f32[1]{0:T(128)}) custom-call(bf16[64,1152]{1,0:T(8,128)(2,1)} %images.1, bf16[64,1152]{1,0:T(8,128)(2,1)} %texts.1, f32[64,1152]{1,0:T(8,128)} %get-tuple-element.8.image_sum, f32[64,1152]{1,0:T(8,128)} %get-tuple-element.9.text_sum, ...), custom_call_target="tpu_custom_call" | custom-call | tf_op jit(solution)/shard_map/finish/pallas_call | solution.py:465
where the time goes:
time: 58.9 us; the launch traced here: 58.8 us
  Pallas kernels  56.9 us (97%)
  between operations  1.93 us (3%)
    pallas_call x1, Pallas kernels, body(): pl.pallas_call(kernel, out_shape=(grad, grad, jax.ShapeDtypeStruct((8, 12...  54.6 us
    pallas_call x1, Pallas kernels, body(): pl.pallas_call(finish, out_shape=(grad, grad, scalar, scalar, scalar), in...  2.26 us

commit v1 on v0

--- a/solution.py
+++ b/solution.py
@@ -20,7 +20,7 @@
     ((0, 1),),
     ((0, 1), (1, 2)),
     ((0, 1), (1, 2), (2, 4)),
-    ((0, 1), (1, 2), (2, 4), (4, 8)),
+    ((0, 1), (1, 2), (2, 4), (4, 6), (6, 8)),
 )
 REDUCE_PARTS = (
     ((1, 2),),
@@ -46,8 +46,8 @@
 
 def decode(y):
     y = y.astype(F32)
-    root = lax.rsqrt(lax.rsqrt(jnp.maximum(jnp.abs(y), 1e-37)))
-    return jnp.where(y > 0.0, root, jnp.where(y < 0.0, -root, 0.0))
+    inverse = lax.rsqrt(jnp.maximum(jnp.abs(y), 1e-37))
+    return y * inverse * inverse * lax.rsqrt(inverse)
 
 
 def kernel(
@@ -88,7 +88,6 @@
     ]
     for c in inputs:
         c.start()
-    sent = []
 
     def copy(src, dst, send, recv, to):
         return pltpu.make_async_remote_copy(
@@ -97,13 +96,12 @@
 
     def start(c):
         c.start()
-        sent.append(c)
 
     def gather_image(q, s, part):
         a, b = GATHER_PARTS[s][part]
         n = FIRST_PART[s] + part
         return copy(
-            img.at[a:b, q], img.at[2**s + a : 2**s + b, q], gi_s.at[q, n], gi_r.at[q, n], plane[(q + s) % 4]
+            img.at[a:b, q], img.at[2**s + a : 2**s + b, q], gi_s, gi_r.at[n], plane[(q + s) % 4]
         )
 
     def gather_text(way, step, half):
@@ -112,30 +110,30 @@
         rows = slice(half * HALF, (half + 1) * HALF)
         return copy(
             txt.at[src, 0, rows], txt.at[dst, 0, rows],
-            gt_s.at[way, step, half], gt_r.at[way, step, half], (above, below)[way],
+            gt_s, gt_r.at[way, step, half], (above, below)[way],
         )
 
     def share_text(slot, half):
         rows = slice(half * HALF, (half + 1) * HALF)
-        return copy(txt.at[slot, 0, rows], txt.at[slot, 1, rows], gc_s.at[slot, half], gc_r.at[slot, half], sibling)
+        return copy(txt.at[slot, 0, rows], txt.at[slot, 1, rows], gc_s, gc_r.at[slot, half], sibling)
 
     def reduce_image(q, s, part):
         a, b = REDUCE_PARTS[s][part]
         n = FIRST_PART[s] + part
-        return copy(isend.at[a:b, q], irecv.at[a:b, q], ri_s.at[q, n], ri_r.at[q, n], plane[(q + s) % 4])
+        return copy(isend.at[a:b, q], irecv.at[a:b, q], ri_s, ri_r.at[n], plane[(q + s) % 4])
 
     def share_sum(slot):
-        return copy(csend.at[slot], crecv.at[slot], rc_s.at[slot], rc_r.at[slot], sibling)
+        return copy(csend.at[slot], crecv.at[slot], rc_s, rc_r.at[slot], sibling)
 
     def reduce_text(way, m, half):
         rows = slice(half * HALF, (half + 1) * HALF)
         return copy(
             tsend.at[way, m, rows], trecv.at[way, m, rows],
-            rt_s.at[way, m, half], rt_r.at[way, m, half], (above, below)[way],
+            rt_s, rt_r.at[way, m, half], (above, below)[way],
         )
 
     def send_stat(n, src, to):
-        return copy(stat.at[src], stat.at[n], st_s.at[n], st_r.at[n], to)
+        return copy(stat.at[src], stat.at[n], st_s, st_r.at[n // 16], to)
 
     inputs[0].wait()
     img[0] = unit_rows(images)[0].astype(BF16).reshape(4, QUARTER, WIDTH)
@@ -209,8 +207,9 @@
         start(share_text(slot, half))
 
     def got_image(s, part):
-        for q in range(4):
-            gather_image(q, s, part).wait_recv()
+        a, b = GATHER_PARTS[s][part]
+        all_four = img.at[2**s + a : 2**s + b]
+        copy(all_four, all_four, gi_s, gi_r.at[FIRST_PART[s] + part], sibling).wait_recv()
 
     def pass_image(stages, part):
         for s in stages:
@@ -226,11 +225,11 @@
     pass_image((1, 2, 3), 1)
     for way in range(2):
         pass_text(way, 0, way)
+    for way in range(2):
+        pass_text(way, 0, 1 - way)
     got_image(1, 0)
     got_image(1, 1)
     pass_image((2, 3), 2)
-    for way in range(2):
-        pass_text(way, 0, 1 - way)
     got_shared((0, 1, 2))
     blocks(0, 4, 0, 3)
     own_pairs()
@@ -241,24 +240,28 @@
     for part in range(3):
         got_image(2, part)
     pass_image((3,), 3)
+    pass_image((3,), 4)
     blocks(4, 8, 0, 3)
     got_shared((3, 4))
     for way in range(2):
         pass_text(way, 2, way)
     blocks(0, 8, 3, 5)
-    for way in range(2):
-        pass_text(way, 2, 1 - way)
     for part in range(3):
         got_image(3, part)
+    for way in range(2):
+        pass_text(way, 2, 1 - way)
     blocks(8, 12, 0, 5)
     got_shared((5, 6))
     blocks(0, 4, 5, 7)
     for way in range(2):
         pass_text(way, 3, way)
     blocks(4, 12, 5, 7)
+    got_image(3, 3)
+    block(12 * ROWS, 128, 0, 896)
+    got_image(3, 4)
+    block(14 * ROWS, 128, 0, 896)
     got_shared((7,))
-    got_image(3, 3)
-    blocks(12, 16, 0, 8)
+    block(0, TILE, 896, 128)
 
     def stat_plane(n):
         return send_stat(n, 0, device((x + n // 4) % 4, (y + n % 4) % 4, z, core))
@@ -274,19 +277,19 @@
             start(stat_plane(n))
 
     def stat_turn():
+        copy(stat.at[1:16], stat.at[1:16], st_s, st_r.at[0], sibling).wait_recv()
         total = stat[0]
         for n in range(1, 16):
-            stat_plane(n).wait_recv()
             total = total + stat[n]
         stat[16] = total
         for n in range(1, 16):
             start(stat_column(n))
 
     def stat_last():
+        copy(stat.at[17:32], stat.at[17:32], st_s, st_r.at[1], sibling).wait_recv()
         total = stat[16]
-        for n in range(1, 16):
-            stat_column(n).wait_recv()
-            total = total + stat[16 + n]
+        for n in range(17, 32):
+            total = total + stat[n]
         stat_sum[...] = total
 
     def image_part(slot):
@@ -312,42 +315,35 @@
                 start(reduce_image(q, s, part))
 
     def wait_images(s, part):
-        for q in range(4):
-            reduce_image(q, s, part).wait_recv()
+        a, b = REDUCE_PARTS[s][part]
+        copy(isend.at[a:b], irecv.at[a:b], ri_s, ri_r.at[FIRST_PART[s] + part], sibling).wait_recv()
 
     def add_images(first, count, stage, forward):
         def one(i, _):
-            slot, q = first + i // 4, i % 4
-            total = iacc[slot, q] + decode(irecv[2**stage + slot, q])
+            slot = first + i
+            total = iacc[slot] + decode(irecv[2**stage + slot])
             if forward:
-                isend[slot, q] = encode(total)
+                isend[slot] = encode(total)
             else:
-                iacc[slot, q] = total
+                iacc[slot] = total
             return 0
 
-        lax.fori_loop(0, 4 * count, one, 0)
+        lax.fori_loop(0, count, one, 0)
 
     def join_texts(slot):
         share_sum(slot).wait_recv()
-
-        def one(i, _):
-            rows = pl.ds(pl.multiple_of(i * 16, 16), 16)
-            tacc[slot, rows] = tacc[slot, rows] + decode(crecv[slot, rows])
-            return 0
-
-        lax.fori_loop(0, 4, one, 0)
+        tacc[slot] = tacc[slot] + decode(crecv[slot])
 
     def pass_sum(way, m, half):
         slot = (DOWN, UP)[way][m]
         arrives = m == 3 and half == way or m < 3
         if arrives:
             reduce_text(way, m + 1, half).wait_recv()
-        for i in range(2):
-            rows = slice(half * HALF + i * 16, half * HALF + (i + 1) * 16)
-            total = tacc[slot, rows]
-            if arrives:
-                total = total + decode(trecv[way, m + 1, rows])
-            tsend[way, m, rows] = encode(total)
+        rows = slice(half * HALF, (half + 1) * HALF)
+        total = tacc[slot, rows]
+        if arrives:
+            total = total + decode(trecv[way, m + 1, rows])
+        tsend[way, m, rows] = encode(total)
         start(reduce_text(way, m, half))
 
     def pass_sums(m, own):
@@ -356,12 +352,11 @@
 
     isend[12:16] = encode(image_part(12))
     send_images(3, (0,))
-    block(0, 768, 896, 128)
     text_part(7, 1)
-    stat_own()
     text_part(5, 2)
     join_texts(7)
     pass_sums(4, True)
+    stat_own()
     isend[8:12] = encode(image_part(8))
     send_images(3, (1, 2, 3))
     join_texts(5)
@@ -370,12 +365,12 @@
     text_part(3, 2)
     iacc[4:8] = image_part(4)
     pass_sums(3, True)
+    wait_images(3, 0)
+    add_images(4, 4, 3, True)
+    send_images(2, (0, 1, 2))
     join_texts(3)
     join_texts(4)
     pass_sums(2, False)
-    wait_images(3, 0)
-    add_images(4, 4, 3, True)
-    send_images(2, (0, 1, 2))
     stat_turn()
     iacc[0:4] = image_part(0)
     text_part(0, 3)
@@ -406,8 +401,16 @@
     text_sum[...] = tacc[0] + decode(trecv[0, 1]) + decode(trecv[1, 1])
     wait_images(0, 0)
     image_sum[...] = (iacc[0] + decode(irecv[1])).reshape(ROWS, WIDTH)
-    for c in sent:
-        c.wait_send()
+    for view, sem in (
+        (img.at[0:15], gi_s),
+        (txt.at[0:7, 0], gt_s),
+        (txt.at[0:8, 0], gc_s),
+        (isend.at[1:16], ri_s),
+        (csend.at[0:8], rc_s),
+        (csend.at[0:7], rt_s),
+        (stat.at[0:30], st_s),
+    ):
+        copy(view, view, sem, in_s.at[0], sibling).wait_send()
 
 
 def finish(images, texts, image_sum, text_sum, stat_sum, log_scale, image_grad, text_grad, loss, scale_grad, bias_grad):
@@ -447,13 +450,13 @@
             pltpu.VMEM((2, 5, ROWS, WIDTH), BF16),
             pltpu.VMEM((33, 8, 128), F32),
             pltpu.VMEM((3, 16, 128), F32),
-            dma((4, 10)), dma((4, 10)),
-            dma((2, 4, 2)), dma((2, 4, 2)),
-            dma((8, 2)), dma((8, 2)),
-            dma((4, 10)), dma((4, 10)),
-            dma((8,)), dma((8,)),
-            dma((2, 5, 2)), dma((2, 5, 2)),
-            dma((32,)), dma((32,)),
+            dma(()), dma((11,)),
+            dma(()), dma((2, 4, 2)),
+            dma(()), dma((8, 2)),
+            dma(()), dma((10,)),
+            dma(()), dma((8,)),
+            dma(()), dma((2, 5, 2)),
+            dma(()), dma((2,)),
             pltpu.VMEM((ROWS, WIDTH), BF16), pltpu.VMEM((ROWS, WIDTH), BF16), dma((2,)),
         ],
         compiler_params=pltpu.CompilerParams(

time: 58.9 us -> 55 us (0.934)
  Pallas kernels: 56.9 us -> 52.9 us
    pallas_call x1, Pallas kernels: 54.6 us -> 50.6 us  [body(): pl.pallas_call(kernel, out_shape=(grad, grad, jax.ShapeDtypeStruct((8, 12...]
where the time goes in v1:
time: 55 us; the launch traced here: 54.8 us
  Pallas kernels  52.9 us (96%)
  between operations  1.93 us (4%)
    pallas_call x1, Pallas kernels, body(): pl.pallas_call(kernel, out_shape=(grad, grad, jax.ShapeDtypeStruct((8, 12...  50.6 us
    pallas_call x1, Pallas kernels, body(): pl.pallas_call(finish, out_shape=(grad, grad, scalar, scalar, scalar), in...  2.26 us

profile of v1, /device:TPU:1, one launch (start us, length us, event | category | flops | bytes accessed | tf_op | source)
XLA Modules:
  0.0 54.8 jit_solution(6798371207213444133)
XLA Ops:
  1.9 50.6 %pairs.1 = (f32[64,1152]{1,0:T(8,128)}, f32[64,1152]{1,0:T(8,128)}, f32[8,128]{1,0:T(8,128)}) custom-call(bf16[64,1152]{1,0:T(8,128)(2,1)} %images.1, bf16[64,1152]{1,0:T(8,128)(2,1)} %texts.1, f32[1,1]{1,0:T(1,128)} %bitcast.2.log_scale, f32[1,1]{1,0:T(1,128)} %bitcast.4.bias), custom_call_target="tpu_custom_call" | custom-call | flops 7247757312 | bytes 1048576 | tf_op jit(solution)/shard_map/pairs/pallas_call | solution.py:434
  52.6 2.3 %finish.1 = (f32[64,1152]{1,0:T(8,128)}, f32[64,1152]{1,0:T(8,128)}, f32[1]{0:T(128)}, f32[1]{0:T(128)}, f32[1]{0:T(128)}) custom-call(bf16[64,1152]{1,0:T(8,128)(2,1)} %images.1, bf16[64,1152]{1,0:T(8,128)(2,1)} %texts.1, f32[64,1152]{1,0:T(8,128)} %get-tuple-element.8.image_sum, f32[64,1152]{1,0:T(8,128)} %get-tuple-element.9.text_sum, ...), custom_call_target="tpu_custom_call" | custom-call | tf_op jit(solution)/shard_map/finish/pallas_call | solution.py:468

commit v2 on v1

--- a/solution.py
+++ b/solution.py
@@ -363,10 +363,9 @@
     join_texts(6)
     pass_sums(3, False)
     text_part(3, 2)
-    iacc[4:8] = image_part(4)
     pass_sums(3, True)
     wait_images(3, 0)
-    add_images(4, 4, 3, True)
+    isend[4:8] = encode(image_part(4) + decode(irecv[12:16]))
     send_images(2, (0, 1, 2))
     join_texts(3)
     join_texts(4)
@@ -377,13 +376,17 @@
     pass_sums(2, True)
     for part in (1, 2, 3):
         wait_images(3, part)
-    add_images(0, 4, 3, False)
-    for slot in (1, 2, 0):
-        join_texts(slot)
+    add_images(2, 2, 3, False)
     wait_images(2, 0)
-    add_images(2, 2, 2, True)
-    send_images(1, (0, 1))
+    add_images(3, 1, 2, True)
+    send_images(1, (0,))
+    add_images(2, 1, 2, True)
+    send_images(1, (1,))
+    join_texts(1)
+    join_texts(2)
     pass_sums(1, False)
+    add_images(0, 2, 3, False)
+    join_texts(0)
     wait_images(2, 1)
     wait_images(2, 2)
     add_images(0, 2, 2, False)

time: 55 us -> 53.9 us (0.980)
  Pallas kernels: 52.9 us -> 51.8 us
    pallas_call x1, Pallas kernels: 50.6 us -> 49.6 us  [body(): pl.pallas_call(kernel, out_shape=(grad, grad, jax.ShapeDtypeStruct((8, 12...]
where the time goes in v2:
time: 53.9 us; the launch traced here: 53.8 us
  Pallas kernels  51.8 us (96%)
  between operations  1.93 us (4%)
    pallas_call x1, Pallas kernels, body(): pl.pallas_call(kernel, out_shape=(grad, grad, jax.ShapeDtypeStruct((8, 12...  49.6 us
    pallas_call x1, Pallas kernels, body(): pl.pallas_call(finish, out_shape=(grad, grad, scalar, scalar, scalar), in...  2.26 us

profile of v2, /device:TPU:1, one launch (start us, length us, event | category | flops | bytes accessed | tf_op | source)
XLA Modules:
  0.0 53.8 jit_solution(2972295850526822623)
XLA Ops:
  1.9 49.6 %pairs.1 = (f32[64,1152]{1,0:T(8,128)}, f32[64,1152]{1,0:T(8,128)}, f32[8,128]{1,0:T(8,128)}) custom-call(bf16[64,1152]{1,0:T(8,128)(2,1)} %images.1, bf16[64,1152]{1,0:T(8,128)(2,1)} %texts.1, f32[1,1]{1,0:T(1,128)} %bitcast.2.log_scale, f32[1,1]{1,0:T(1,128)} %bitcast.4.bias), custom_call_target="tpu_custom_call" | custom-call | flops 7247757312 | bytes 1048576 | tf_op jit(solution)/shard_map/pairs/pallas_call | solution.py:437
  51.5 2.3 %finish.1 = (f32[64,1152]{1,0:T(8,128)}, f32[64,1152]{1,0:T(8,128)}, f32[1]{0:T(128)}, f32[1]{0:T(128)}, f32[1]{0:T(128)}) custom-call(bf16[64,1152]{1,0:T(8,128)(2,1)} %images.1, bf16[64,1152]{1,0:T(8,128)(2,1)} %texts.1, f32[64,1152]{1,0:T(8,128)} %get-tuple-element.8.image_sum, f32[64,1152]{1,0:T(8,128)} %get-tuple-element.9.text_sum, ...), custom_call_target="tpu_custom_call" | custom-call | tf_op jit(solution)/shard_map/finish/pallas_call | solution.py:471

commit v3 on v2

--- a/solution.py
+++ b/solution.py
@@ -371,12 +371,11 @@
     join_texts(4)
     pass_sums(2, False)
     stat_turn()
-    iacc[0:4] = image_part(0)
     text_part(0, 3)
     pass_sums(2, True)
     for part in (1, 2, 3):
         wait_images(3, part)
-    add_images(2, 2, 3, False)
+    iacc[0:4] = image_part(0) + decode(irecv[8:12])
     wait_images(2, 0)
     add_images(3, 1, 2, True)
     send_images(1, (0,))
@@ -385,7 +384,6 @@
     join_texts(1)
     join_texts(2)
     pass_sums(1, False)
-    add_images(0, 2, 3, False)
     join_texts(0)
     wait_images(2, 1)
     wait_images(2, 2)

time: 53.9 us -> 54.1 us (level)
  no operation moved by 1% of the time
where the time goes in v3:
time: 54.1 us; the launch traced here: 53.7 us
  Pallas kernels  51.8 us (96%)
  between operations  1.93 us (4%)
    pallas_call x1, Pallas kernels, body(): pl.pallas_call(kernel, out_shape=(grad, grad, jax.ShapeDtypeStruct((8, 12...  49.5 us
    pallas_call x1, Pallas kernels, body(): pl.pallas_call(finish, out_shape=(grad, grad, scalar, scalar, scalar), in...  2.26 us

profile of v3, /device:TPU:1, one launch (start us, length us, event | category | flops | bytes accessed | tf_op | source)
XLA Modules:
  0.0 53.7 jit_solution(9996337168437006324)
XLA Ops:
  1.9 49.5 %pairs.1 = (f32[64,1152]{1,0:T(8,128)}, f32[64,1152]{1,0:T(8,128)}, f32[8,128]{1,0:T(8,128)}) custom-call(bf16[64,1152]{1,0:T(8,128)(2,1)} %images.1, bf16[64,1152]{1,0:T(8,128)(2,1)} %texts.1, f32[1,1]{1,0:T(1,128)} %bitcast.2.log_scale, f32[1,1]{1,0:T(1,128)} %bitcast.4.bias), custom_call_target="tpu_custom_call" | custom-call | flops 7247757312 | bytes 1048576 | tf_op jit(solution)/shard_map/pairs/pallas_call | solution.py:435
  51.4 2.3 %finish.1 = (f32[64,1152]{1,0:T(8,128)}, f32[64,1152]{1,0:T(8,128)}, f32[1]{0:T(128)}, f32[1]{0:T(128)}, f32[1]{0:T(128)}) custom-call(bf16[64,1152]{1,0:T(8,128)(2,1)} %images.1, bf16[64,1152]{1,0:T(8,128)(2,1)} %texts.1, f32[64,1152]{1,0:T(8,128)} %get-tuple-element.8.image_sum, f32[64,1152]{1,0:T(8,128)} %get-tuple-element.9.text_sum, ...), custom_call_target="tpu_custom_call" | custom-call | tf_op jit(solution)/shard_map/finish/pallas_call | solution.py:469
